TPU v7x, 256 devices: a whole 4x4x8 slice. The times are simulated.
256 devices in a mesh: sec: 64 (over x, z, core), env: 4 (over y).
Axes of the slice: x: 4, y: 4, z: 8, core: 2. Of those that a mesh axis runs over, the one named last changes fastest.
Arguments:
- wavefunction: float32 [256, 256, 256], P('sec', 'env'), as said below
- left_env: bfloat16 [256, 16, 256, 256], P('sec', None, 'env'), may hold values from -0.375 to 0.375
- right_env: bfloat16 [256, 16, 256, 256], P('sec'), may hold values from -0.375 to 0.375
- shifts: int32 [16], replicated, may hold values from -2 to 2, as said below
- block_dims: int32 [256, 2], P('sec'), may hold values from 128 to 256, as said below
- precond: float32 [256, 256], P('sec', 'env'), may hold values from 0.5 to 4
Outputs:
- ritz_vector: float32 [256, 256, 256], P('sec', 'env')
- ritz_values: float32 [2], replicated
Inputs may be any that keep to these rules, and one draw needn't show every extreme that they name: Term w of sector s reads the block of sector s + shifts[w]. `block_dims`: entries of a block beyond these dimensions are padding. `wavefunction`: a real field; sectors differ in scale.
All inputs are finite; a program needn't handle non-finite values.
Results may differ from a plain program's by a relative error of at most 0.0041.
Values may be sent and summed in bfloat16 or wider, within the bound.
A program may use at most 64 MiB of HBM per device.

v0:
```python
import jax
import jax.numpy as jnp
from jax import lax
from jax.sharding import PartitionSpec as P

MAXSHIFT = 2
ITERS = 2


def padded(block, sides, width):
    for axis, dim in sides:
        count = lax.axis_size(axis)
        forward = [(i, i + 1) for i in range(count - 1)]
        backward = [(target, source) for source, target in forward]
        low = lax.ppermute(
            lax.slice_in_dim(block, block.shape[dim] - width, None, axis=dim), axis, forward
        )
        high = lax.ppermute(lax.slice_in_dim(block, 0, width, axis=dim), axis, backward)
        block = jnp.concatenate([low, block, high], axis=dim)
    return block


def local(wavefunction, left_env, right_env, shifts, block_dims, precond):
    sectors, rows, cols = wavefunction.shape
    terms = left_env.shape[1]
    count = float(sectors * rows * cols * lax.axis_size("sec") * lax.axis_size("env"))
    row_ids = lax.axis_index("env") * rows + jnp.arange(rows, dtype=jnp.int32)
    col_ids = jnp.arange(cols, dtype=jnp.int32)
    rows_ok = row_ids[None, :] < block_dims[:, 0:1]
    cols_ok = col_ids[None, :] < block_dims[:, 1:2]
    live = (rows_ok[:, :, None] & cols_ok[:, None, :]).astype(jnp.float32)

    def local_product(first, second):
        return jnp.sum(first * second) / count

    def apply_hamiltonian(vector):
        narrow = vector.astype(jnp.bfloat16)
        whole = lax.all_gather(narrow, "env", axis=1, tiled=True)
        widened = padded(whole, (("sec", 0),), MAXSHIFT)
        total = jnp.zeros((sectors, rows, cols), jnp.float32)
        for term_no in range(terms):
            start_at = shifts[term_no] + MAXSHIFT
            source = lax.dynamic_slice_in_dim(widened, start_at, sectors, 0)
            partial_rows = jnp.einsum(
                "sij,sjk->sik", left_env[:, term_no], source, preferred_element_type=jnp.float32
            ).astype(jnp.bfloat16)
            total = total + jnp.einsum(
                "sij,sjk->sik",
                partial_rows,
                right_env[:, term_no],
                preferred_element_type=jnp.float32,
            )
        return total * live

    start = wavefunction * live
    start_sq = lax.psum(local_product(start, start), ("sec", "env"))
    vector = start * lax.rsqrt(start_sq + 1e-06)
    applied = apply_hamiltonian(vector)
    values = []
    for step in range(ITERS):
        rayleigh = lax.psum(local_product(vector, applied), ("sec", "env"))
        correction = (applied - rayleigh * vector) / precond[:, :, None]
        along = lax.psum(local_product(vector, correction), ("sec", "env"))
        correction = correction - along * vector
        corr_sq = lax.psum(local_product(correction, correction), ("sec", "env"))
        unit = correction * lax.rsqrt(corr_sq + 1e-06)
        applied_unit = apply_hamiltonian(unit)
        first_coupling, second_coupling, upper = lax.psum(
            (
                local_product(unit, applied),
                local_product(vector, applied_unit),
                local_product(unit, applied_unit),
            ),
            ("sec", "env"),
        )
        coupling = 0.5 * (first_coupling + second_coupling)
        angle = 0.5 * jnp.arctan2(-2.0 * coupling, upper - rayleigh)
        values.append(
            0.5 * (rayleigh + upper) - jnp.sqrt(0.25 * (rayleigh - upper) ** 2 + coupling**2)
        )
        cosine = jnp.cos(angle)
        sine_t = jnp.sin(angle)
        vector = cosine * vector + sine_t * unit
        applied = cosine * applied + sine_t * applied_unit
    return (vector, jnp.stack(values))


def solution(mesh):
    in_specs = (
        P("sec", "env", None),
        P("sec", None, "env", None),
        P("sec", None, None, None),
        P(),
        P("sec", None),
        P("sec", "env"),
    )
    out_specs = (P("sec", "env", None), P())
    return jax.shard_map(local, mesh=mesh, in_specs=in_specs, out_specs=out_specs, check_vma=False)
```

profile of v0, /device:TPU:1, one launch (start us, length us, event | category | flops | bytes accessed | tf_op | source)
XLA Modules:
  0.0 902.7 jit_solution(12375073013106048321)
XLA Ops:
  3.9 81.4 %psum.91 = f32[]{:T(128)} all-reduce(f32[]{:T(128)S(6)} %div.53), channel_id=1, replica_groups=mesh['sec'=64,'env'=4] {'sec','env'}, use_global_device_ids=true, to_apply=%region_1.0 | all-reduce | flops 1 | bytes 8 | tf_op jit(solution)/shard_map/psum | solution.py:56
  87.0 10.0 %all_gather.9 = bf16[4,256,256]{2,1,0:T(8,128)(2,1)S(1)} all-gather(bf16[4,64,256]{2,1,0:T(8,128)(2,1)S(1)} %fusion.391), channel_id=1, replica_groups=mesh['sec'=64,'env'=4] {'env'}, dimensions={1}, use_global_device_ids=true | all-gather | bytes 655360 | tf_op jit(solution)/shard_map/all_gather | solution.py:38
  98.6 6.8 collective-permute-start
  153.8 2.2 convolution_add_fusion.32
  156.0 2.2 convolution_add_fusion.31
  158.1 2.7 multiply_reduce_fusion.11
  161.5 74.1 %psum.92 = f32[]{:T(128)} all-reduce(f32[]{:T(128)S(6)} %div.54), channel_id=1, replica_groups=mesh['sec'=64,'env'=4] {'sec','env'}, use_global_device_ids=true, to_apply=%region_3.0 | all-reduce | flops 1 | bytes 8 | tf_op jit(solution)/shard_map/psum | solution.py:61
  235.6 2.5 multiply_reduce_fusion.10
  238.8 73.5 %psum.93 = f32[]{:T(128)} all-reduce(f32[]{:T(128)S(6)} %div.57), channel_id=1, replica_groups=mesh['sec'=64,'env'=4] {'sec','env'}, use_global_device_ids=true, to_apply=%region_5.0 | all-reduce | flops 1 | bytes 8 | tf_op jit(solution)/shard_map/psum | solution.py:63
  312.2 3.1 multiply_reduce_fusion.9
  316.0 73.4 %psum.94 = f32[]{:T(128)} all-reduce(f32[]{:T(128)S(6)} %div.58), channel_id=1, replica_groups=mesh['sec'=64,'env'=4] {'sec','env'}, use_global_device_ids=true, to_apply=%region_7.0 | all-reduce | flops 1 | bytes 8 | tf_op jit(solution)/shard_map/psum | solution.py:65
  390.1 11.3 %all_gather.10 = bf16[4,256,256]{2,1,0:T(8,128)(2,1)S(1)} all-gather(bf16[4,64,256]{2,1,0:T(8,128)(2,1)S(1)} %multiply_convert_fusion.1), channel_id=1, replica_groups=mesh['sec'=64,'env'=4] {'env'}, dimensions={1}, use_global_device_ids=true | all-gather | bytes 655360 | tf_op jit(solution)/shard_map/all_gather | solution.py:38
  401.4 5.4 collective-permute-start.2
  410.1 4.3 collective-permute-done.3
  446.5 3.0 multiply_reduce_fusion.6
  451.4 77.4 %all-reduce.1 = (f32[]{:T(128)}, f32[]{:T(128)}) all-reduce(f32[]{:T(128)S(6)} %multiply.25, f32[]{:T(128)S(6)} %div.61), channel_id=1, replica_groups=mesh['sec'=64,'env'=4] {'sec','env'}, use_global_device_ids=true, to_apply=%region_9.0 | all-reduce | flops 2 | bytes 16 | tf_op jit(solution)/shard_map/psum | solution.py:68
  533.6 72.4 %psum.98 = f32[]{:T(128)} all-reduce(f32[]{:T(128)S(6)} %div.62), channel_id=1, replica_groups=mesh['sec'=64,'env'=4] {'sec','env'}, use_global_device_ids=true, to_apply=%region_15.0 | all-reduce | flops 1 | bytes 8 | tf_op jit(solution)/shard_map/psum | solution.py:61
  608.1 73.7 %psum.99 = f32[]{:T(128)} all-reduce(f32[]{:T(128)S(6)} %div.64), channel_id=1, replica_groups=mesh['sec'=64,'env'=4] {'sec','env'}, use_global_device_ids=true, to_apply=%region_17.0 | all-reduce | flops 1 | bytes 8 | tf_op jit(solution)/shard_map/psum | solution.py:63
  684.4 73.4 %psum.100 = f32[]{:T(128)} all-reduce(f32[]{:T(128)S(6)} %div.65), channel_id=1, replica_groups=mesh['sec'=64,'env'=4] {'sec','env'}, use_global_device_ids=true, to_apply=%region_19.0 | all-reduce | flops 1 | bytes 8 | tf_op jit(solution)/shard_map/psum | solution.py:65
  758.6 11.1 %all_gather.11 = bf16[4,256,256]{2,1,0:T(8,128)(2,1)S(1)} all-gather(bf16[4,64,256]{2,1,0:T(8,128)(2,1)S(1)} %multiply_convert_fusion), channel_id=1, replica_groups=mesh['sec'=64,'env'=4] {'env'}, dimensions={1}, use_global_device_ids=true | all-gather | bytes 655360 | tf_op jit(solution)/shard_map/all_gather | solution.py:38
  771.2 5.9 collective-permute-start.4
  809.3 2.2 convolution_add_fusion.2
  813.6 2.3 multiply_reduce_fusion
  817.8 76.8 %all-reduce = (f32[]{:T(128)}, f32[]{:T(128)}) all-reduce(f32[]{:T(128)S(6)} %multiply.26, f32[]{:T(128)S(6)} %div.68), channel_id=1, replica_groups=mesh['sec'=64,'env'=4] {'sec','env'}, use_global_device_ids=true, to_apply=%region_21.0 | all-reduce | flops 2 | bytes 16 | tf_op jit(solution)/shard_map/psum | solution.py:68
  (98 shorter events, 107.8 us)
Async XLA Ops:
  0.6 106.7 %copy-start.9 = (s32[16]{0:T(128)S(1)}, s32[16]{0:T(128)}, u32[]{:S(2)}) copy-start(s32[16]{0:T(128)} %param.9) | copy-start | bytes 196
  87.0 43.5 %copy-start = (bf16[4,16,64,256]{3,2,1,0:T(8,128)(2,1)S(1)}, bf16[4,16,64,256]{3,2,1,0:T(8,128)(2,1)}, u32[]{:S(2)}) copy-start(bf16[4,16,64,256]{3,2,1,0:T(8,128)(2,1)} %param.7) | copy-start | bytes 6291460
  97.1 0.8 copy-start.4
  98.6 29.8 %collective-permute-start = (bf16[2,256,256]{2,1,0:T(8,128)(2,1)S(1)}, bf16[2,256,256]{2,1,0:T(8,128)(2,1)}, u32[]{:S(2)}, u32[]{:S(2)}) collective-permute-start(bf16[2,256,256]{2,1,0:T(8,128)(2,1)S(1)} %get-tuple-element.24), channel_id=1, source_target_pairs={{0,4},{4,8},{8,12},{12,16},{16,20},{20,24},{24,28},{28,32},{32,36}... | collective-permute-start | bytes 786440 | tf_op jit(solution)/shard_map/ppermute | solution.py:15
  105.4 25.1 %collective-permute-start.1 = (bf16[2,256,256]{2,1,0:T(8,128)(2,1)}, bf16[2,256,256]{2,1,0:T(8,128)(2,1)S(1)}, u32[]{:S(2)}, u32[]{:S(2)}) collective-permute-start(bf16[2,256,256]{2,1,0:T(8,128)(2,1)} %get-tuple-element.23), channel_id=1, source_target_pairs={{4,0},{8,4},{12,8},{16,12},{20,16},{24,20},{28,24},{32,28},{36,32}... | collective-permute-start | bytes 786440 | tf_op jit(solution)/shard_map/ppermute | solution.py:18
  153.8 4.3 copy-start.1
  156.0 79.6 %copy-start.10 = (f32[4,64]{1,0:T(4,128)S(1)}, f32[4,64]{1,0:T(4,128)}, u32[]{:S(2)}) copy-start(f32[4,64]{1,0:T(4,128)} %param.11) | copy-start | bytes 3076
  315.4 93.3 %copy-start.8 = (f32[4,64,256]{2,1,0:T(8,128)}, f32[4,64,256]{2,1,0:T(8,128)S(1)}, u32[]{:S(2)}) copy-start(f32[4,64,256]{2,1,0:T(8,128)S(1)} %get-tuple-element.18) | copy-start | bytes 786436
  401.4 8.7 collective-permute-start.2
  406.8 7.7 collective-permute-start.3
  533.0 250.1 %copy-start.2 = (f32[4,64,256]{2,1,0:T(8,128)}, f32[4,64,256]{2,1,0:T(8,128)S(1)}, u32[]{:S(2)}) copy-start(f32[4,64,256]{2,1,0:T(8,128)S(1)} %get-tuple-element.16) | copy-start | bytes 786436
  533.0 250.1 %copy-start.7 = (f32[4,64,256]{2,1,0:T(8,128)}, f32[4,64,256]{2,1,0:T(8,128)S(1)}, u32[]{:S(2)}) copy-start(f32[4,64,256]{2,1,0:T(8,128)S(1)} %get-tuple-element.15) | copy-start | bytes 786436
  683.7 102.4 %copy-start.6 = (f32[4,64,256]{2,1,0:T(8,128)}, f32[4,64,256]{2,1,0:T(8,128)S(1)}, u32[]{:S(2)}) copy-start(f32[4,64,256]{2,1,0:T(8,128)S(1)} %get-tuple-element.13) | copy-start | bytes 786436
  769.6 0.8 copy-start.5
  771.2 11.9 %collective-permute-start.4 = (bf16[2,256,256]{2,1,0:T(8,128)(2,1)S(1)}, bf16[2,256,256]{2,1,0:T(8,128)(2,1)}, u32[]{:S(2)}, u32[]{:S(2)}) collective-permute-start(bf16[2,256,256]{2,1,0:T(8,128)(2,1)S(1)} %get-tuple-element.20), channel_id=1, source_target_pairs={{0,4},{4,8},{8,12},{12,16},{16,20},{20,24},{24,28},{28,32},{32,36}... | collective-permute-start | bytes 786440 | tf_op jit(solution)/shard_map/ppermute | solution.py:15
  777.1 8.1 collective-permute-start.5
  809.3 4.3 copy-start.3
where the time goes:
time: 906 us; the launch traced here: 903 us
  blocking collectives  708 us (78%)
  matrix products  94.9 us (10%)
  between operations  44.1 us (5%)
  starting transfers between devices  23.8 us (3%)
  other arithmetic  16.1 us (2%)
  local copies, waits for them, and re-layouts  9.77 us (1%)
    psum x2, blocking collectives, local(): lax.psum((local_product(unit, applied), local_product(vector, applied_uni...  154 us
    psum x2, blocking collectives, local(): along = lax.psum(local_product(vector, correction), ('sec', 'env'))  147 us
    psum x2, blocking collectives, local(): corr_sq = lax.psum(local_product(correction, correction), ('sec', 'env'))  147 us
    psum x2, blocking collectives, local(): rayleigh = lax.psum(local_product(vector, applied), ('sec', 'env'))  146 us
    dot_general x48, matrix products, apply_hamiltonian(): jnp.einsum('sij,sjk->sik', partial_rows, right_env[:, term_no], preferred...  94.9 us
    psum x1, blocking collectives, local(): start_sq = lax.psum(local_product(start, start), ('sec', 'env'))  81.4 us
    all_gather x3, blocking collectives, apply_hamiltonian(): whole = lax.all_gather(narrow, 'env', axis=1, tiled=True)  32.4 us
  transfers between devices with their start and end apart: 6, of which 2 were waited for; matrix products, arithmetic and copies ran while one was open for 1% of the time, Pallas kernels for 0%

commit v1 on v0

v1 whole, which is shorter than its diff:
```python
import jax
import jax.numpy as jnp
from jax import lax
from jax.experimental import pallas as pl
from jax.experimental.pallas import tpu as pltpu
from jax.sharding import PartitionSpec as P

MAXSHIFT = 2
BF = jnp.bfloat16
F32 = jnp.float32
MESH = pl.DeviceIdType.MESH
ENV = 4
LANES = 128


def dot(a, b):
    return jnp.dot(a, b, preferred_element_type=F32)


def make_kernel(nsec, sectors, terms, rows, cols):
    zs = 8 if nsec % 16 == 0 else 2
    xs = nsec // (2 * zs)
    near = 2 * ENV * xs
    wide = sectors + 2 * MAXSHIFT
    count = float(nsec * sectors * ENV * rows * cols)

    def kernel(
        shifts, dims, wf, prec, left_hbm, right_hbm, out, ritz,
        left, right, xs_buf, xd_buf, xq_buf, xt_buf, dall, dpad, dcol, dinv,
        live, start, va, vda, vh, vq, vc, near_slots, far_slots, total,
        load_sem, go_sem, gi_sem, out_sem, in_sem, send_sem, d_send, d_recv,
        near_send, near_recv, far_send, far_recv,
    ):
        sec = lax.axis_index("sec")
        y = lax.axis_index("env")
        core = lax.rem(sec, 2)
        chip = sec // 2
        z = lax.rem(chip, zs)
        x = chip // zs
        has_out = jnp.logical_or(
            jnp.logical_and(core == 0, sec > 0), jnp.logical_and(core == 1, sec < nsec - 1)
        )
        outer = jnp.clip(sec + 2 * core - 1, 0, nsec - 1)
        inner = sec + 1 - 2 * core
        out_src, out_dst = 2 * core, 6 * (1 - core)
        in_src, in_dst = 2 * (1 - core), 6 * core

        def yy(k):
            return lax.rem(y + k + ENV, ENV)

        near_rank = (core * ENV + y) * xs + x

        def near_peer(k):
            m = lax.rem(near_rank + k, near)
            return (((lax.rem(m, xs) * zs + z) * 2 + m // (xs * ENV)), lax.rem(m // xs, ENV))

        def far_peer(k):
            m = lax.rem(z + k, zs)
            return (((x * zs + m) * 2 + core), y)

        load_left = pltpu.make_async_copy(left_hbm, left, load_sem.at[0])
        load_right = pltpu.make_async_copy(right_hbm, right, load_sem.at[1])
        load_left.start()
        load_right.start()

        zero = jnp.zeros((MAXSHIFT, ENV, rows, cols), BF)
        ones = jnp.ones((MAXSHIFT, ENV, 1, LANES), F32)

        @pl.when(sec == 0)
        def _():
            for buf in (xs_buf, xd_buf, xq_buf):
                buf[0:MAXSHIFT] = zero
            dall[0:MAXSHIFT] = ones

        @pl.when(sec == nsec - 1)
        def _():
            for buf in (xs_buf, xd_buf, xq_buf):
                buf[wide - MAXSHIFT : wide] = zero
            dall[wide - MAXSHIFT : wide] = ones

        barrier = pltpu.get_barrier_semaphore()
        for k in range(1, near):
            pl.semaphore_signal(barrier, inc=1, device_id=near_peer(k), device_id_type=MESH)
        for k in range(1, zs):
            pl.semaphore_signal(barrier, inc=1, device_id=far_peer(k), device_id_type=MESH)

        @pl.when(has_out)
        def _():
            for k in range(ENV):
                pl.semaphore_signal(barrier, inc=1, device_id=(outer, yy(k)), device_id_type=MESH)

        row_ids = y * rows + lax.broadcasted_iota(jnp.int32, (rows, cols), 0)
        col_ids = lax.broadcasted_iota(jnp.int32, (rows, cols), 1)
        own = pl.ds(MAXSHIFT, sectors)
        sq = jnp.zeros((rows, cols), F32)
        for s in range(sectors):
            ok = jnp.logical_and(row_ids < dims[s, 0], col_ids < dims[s, 1])
            mask = jnp.where(ok, 1.0, 0.0).astype(F32)
            live[s] = mask
            st = wf[s] * mask
            start[s] = st
            xs_buf[MAXSHIFT + s, y] = st.astype(BF)
            sq = sq + st * st
            dall[MAXSHIFT + s, y, :, 0:rows] = prec[s : s + 1, :]

        def fold(v):
            w = jnp.sum(v.reshape(rows // 8, 8, cols), axis=0)
            t = w[:, 0:LANES]
            for c in range(1, cols // LANES):
                t = t + w[:, c * LANES : (c + 1) * LANES]
            return jnp.sum(t, axis=0, keepdims=True)

        pl.semaphore_wait(barrier, near - 1 + zs - 1 + jnp.where(has_out, ENV, 0))

        def cp(src, dst, ss, rs, dev):
            return pltpu.make_async_remote_copy(
                src_ref=src, dst_ref=dst, send_sem=ss, recv_sem=rs, device_id=dev, device_id_type=MESH
            )

        ORDER = (1, 3, 2)

        def gather_outer(e, buf, k):
            part = buf.at[pl.ds(MAXSHIFT + out_src, 2), y]
            return cp(part, part, send_sem.at[e, 0, k], go_sem.at[e, k], (sec, yy(k)))

        def gather_inner(e, buf, k):
            part = buf.at[pl.ds(MAXSHIFT + in_src, 2), y]
            return cp(part, part, send_sem.at[e, 1, k], gi_sem.at[e, k], (sec, yy(k)))

        def relay_outer(e, buf, k):
            p = yy(-k)
            src = buf.at[pl.ds(MAXSHIFT + out_src, 2), p]
            dst = buf.at[pl.ds(out_dst, 2), p]
            return cp(src, dst, send_sem.at[e, 2, k], out_sem.at[e, k], (outer, y))

        def relay_inner(e, buf, k):
            p = yy(-k)
            src = buf.at[pl.ds(MAXSHIFT + in_src, 2), p]
            dst = buf.at[pl.ds(in_dst, 2), p]
            return cp(src, dst, send_sem.at[e, 3, k], in_sem.at[e, k], (inner, y))

        def begin(e, buf):
            @pl.when(has_out)
            def _():
                relay_outer(e, buf, 0).start()

            for k in ORDER:
                gather_outer(e, buf, k).start()
            relay_inner(e, buf, 0).start()
            for k in ORDER:
                gather_inner(e, buf, k).start()

        def relay(e, buf):
            for k in ORDER:
                gather_outer(e, buf, k).wait_recv()

                @pl.when(has_out)
                def _():
                    relay_outer(e, buf, k).start()

            for k in ORDER:
                gather_inner(e, buf, k).wait_recv()
                relay_inner(e, buf, k).start()

        def finish(e, buf):
            for k in (0,) + ORDER:
                relay_inner(e, buf, k).wait_recv()

            @pl.when(has_out)
            def _():
                for k in (0,) + ORDER:
                    relay_outer(e, buf, k).wait_recv()

        def drain(e, buf):
            for k in ORDER:
                gather_outer(e, buf, k).wait_send()
                gather_inner(e, buf, k).wait_send()
            for k in (0,) + ORDER:
                relay_inner(e, buf, k).wait_send()

            @pl.when(has_out)
            def _():
                for k in (0,) + ORDER:
                    relay_outer(e, buf, k).wait_send()

        def near_copy(r, k):
            ref = near_slots.at[r, near_rank]
            return cp(ref, ref, near_send.at[r], near_recv.at[r], near_peer(k))

        def far_copy(r, k):
            ref = far_slots.at[r, z]
            return cp(ref, ref, far_send.at[r], far_recv.at[r], far_peer(k))

        def near_all(r):
            ref = near_slots.at[r, pl.ds(0, near - 1)]
            return cp(ref, ref, near_send.at[r], near_recv.at[r], near_peer(1))

        def far_all(r):
            ref = far_slots.at[r, pl.ds(0, zs - 1)]
            return cp(ref, ref, far_send.at[r], far_recv.at[r], far_peer(1))

        def sum_begin(r, parts):
            parts = parts + [jnp.zeros((1, LANES), F32)] * (8 - len(parts))
            near_slots[r, near_rank] = jnp.concatenate(parts, axis=0)
            for k in range(1, near):
                near_copy(r, k).start()

        def sum_middle(r):
            near_all(r).wait_recv()
            far_slots[r, z] = jnp.sum(near_slots[r], axis=0)
            for k in range(1, zs):
                far_copy(r, k).start()

        def sum_end(r):
            far_all(r).wait_recv()
            t = jnp.sum(far_slots[r], axis=0)
            t = jnp.sum(t, axis=1, keepdims=True) * (1.0 / count)
            return jnp.broadcast_to(t, (8, LANES))

        def sum_drain(r):
            near_all(r).wait_send()
            far_all(r).wait_send()

        def row(t, i):
            return t[i : i + 1, :]

        def scalar(r):
            return r[0, 0]

        def apply(buf, done):
            def body(s, carry):
                acc = jnp.zeros((rows, cols), F32)
                for w in range(terms):
                    source = buf[s + MAXSHIFT + shifts[w]].reshape(ENV * rows, cols)
                    part = dot(left[s, w], source).astype(BF)
                    acc = acc + dot(part, right[s, w])
                return done(s, acc, carry)

            return body

        def over_sectors(body, init):
            return lax.fori_loop(0, sectors, body, init)

        def zeros(n):
            return tuple(jnp.zeros((1, LANES), F32) for _ in range(n))

        begin(0, xs_buf)
        sum_begin(0, [fold(sq)])

        def d_copies():
            piece = dall.at[own, y]
            res = [cp(piece, piece, d_send.at[0, k], d_recv.at[0, k], (sec, yy(k))) for k in range(1, ENV)]
            for k in range(ENV):
                src = dall.at[pl.ds(MAXSHIFT + in_src, 2), y]
                dst = dall.at[pl.ds(in_dst, 2), y]
                res.append(cp(src, dst, d_send.at[1, k], d_recv.at[1, k], (inner, yy(k))))
            return res

        def d_outer():
            res = []
            for k in range(ENV):
                src = dall.at[pl.ds(MAXSHIFT + out_src, 2), y]
                dst = dall.at[pl.ds(out_dst, 2), y]
                res.append(cp(src, dst, d_send.at[2, k], d_recv.at[2, k], (outer, yy(k))))
            return res

        for c in d_copies():
            c.start()

        @pl.when(has_out)
        def _():
            for c in d_outer():
                c.start()

        relay(0, xs_buf)
        sum_middle(0)
        load_left.wait()
        load_right.wait()
        for c in d_copies():
            c.wait_recv()

        @pl.when(has_out)
        def _():
            for c in d_outer():
                c.wait_recv()

        dpad[...] = jnp.ones((LANES, LANES), F32)
        for s in range(wide):
            for e in range(ENV):
                dpad[s * ENV + e : s * ENV + e + 1, 0:rows] = dall[s, e, :, 0:rows]
        dcol[...] = 1.0 / jnp.transpose(dpad[...])
        for s in range(sectors):
            rowd = jnp.zeros((1, LANES), F32)
            for e in range(ENV):
                rowd = jnp.where(y == e, dpad[(MAXSHIFT + s) * ENV + e : (MAXSHIFT + s) * ENV + e + 1, :], rowd)
            dpad[64 + s : 65 + s, :] = rowd
        mine = 1.0 / jnp.transpose(dpad[...])
        for s in range(sectors):
            dinv[s] = jnp.broadcast_to(mine[0:rows, 64 + s : 65 + s], (rows, cols))

        sum_end0 = sum_end(0)
        c0 = lax.rsqrt(row(sum_end0, 0) + 1e-06)
        c0s = scalar(c0)
        finish(0, xs_buf)

        def done0(s, acc, carry):
            a = acc * live[s] * c0s
            v = start[s] * c0s
            start[s] = v
            va[s] = a
            di = dinv[s]
            da = a * di
            vda[s] = da
            xd_buf[s + MAXSHIFT, y] = da.astype(BF)
            return (carry[0] + fold(v * a), carry[1] + fold(v * da), carry[2] + fold(v * (v * di)))

        sums = over_sectors(apply(xs_buf, done0), zeros(3))

        begin(1, xd_buf)
        sum_begin(1, list(sums))

        def scale_start(s, carry):
            for e in range(ENV):
                col = jnp.zeros((rows, 1), F32)
                col = dcol_of(s, e)
                xt_buf[s, e] = (xs_buf[s, e].astype(F32) * col * c0s).astype(BF)
            return carry

        def dcol_of(s, e):
            lane = lax.broadcasted_iota(jnp.int32, (rows, LANES), 1)
            hit = jnp.where(lane == s * ENV + e, dcol[0:rows, :], 0.0)
            return jnp.sum(hit, axis=1, keepdims=True)

        lax.fori_loop(0, wide, scale_start, 0)
        relay(1, xd_buf)
        sum_middle(1)

        def done_h(s, acc, carry):
            vh[s] = acc * live[s]
            return carry

        over_sectors(apply(xt_buf, done_h), 0)
        sum1 = sum_end(1)
        r0 = row(sum1, 0)
        along0 = row(sum1, 1) - r0 * row(sum1, 2)
        r0s, along0s = scalar(r0), scalar(along0)
        finish(1, xd_buf)

        def done1(s, acc, carry):
            a, v, di, da = va[s], start[s], dinv[s], vda[s]
            q = acc * live[s] - r0s * vh[s] - along0s * a
            corr = da - r0s * (v * di) - along0s * v
            vq[s] = q
            vc[s] = corr
            xq_buf[s + MAXSHIFT, y] = q.astype(BF)
            dq, dc = q * di, corr * di
            new = (
                corr * corr, corr * a, v * q, corr * q,
                v * dq + corr * da, corr * dq, v * dc, corr * dc,
            )
            return tuple(c + fold(n) for c, n in zip(carry, new, strict=True))

        sums = over_sectors(apply(xd_buf, done1), zeros(8))

        begin(2, xq_buf)
        sum_begin(2, list(sums))
        relay(2, xq_buf)
        sum_middle(2)
        t = sum_end(2)
        sum1_vda, sum1_vdv = row(sum1, 1), row(sum1, 2)

        def rotation(rayleigh, upper, coupling):
            px, py = upper - rayleigh, -2.0 * coupling
            big = jnp.maximum(jnp.abs(px), jnp.abs(py))
            safe = jnp.where(big > 0.0, big, 1.0)
            ux, uy = px / safe, py / safe
            h = jnp.sqrt(ux * ux + uy * uy)
            h = jnp.where(big > 0.0, h, 1.0)
            ux = jnp.where(big > 0.0, ux, 1.0)
            large = jnp.sqrt(0.5 * (1.0 + jnp.abs(ux) / h))
            small = jnp.abs(uy) / (2.0 * h * large)
            cosine = jnp.where(ux >= 0.0, large, small)
            sine = jnp.where(ux >= 0.0, small, large)
            sine = jnp.where(uy > 0.0, sine, -sine)
            half = 0.5 * (rayleigh - upper)
            ritz_value = 0.5 * (rayleigh + upper) - jnp.sqrt(half * half + coupling * coupling)
            return cosine, sine, ritz_value

        alpha = lax.rsqrt(row(t, 0) + 1e-06)
        cross = row(t, 1) + row(t, 2)
        coupling = 0.5 * alpha * cross
        upper = alpha * alpha * row(t, 3)
        cosine, sine, value0 = rotation(r0, upper, coupling)
        sa = sine * alpha
        r1 = cosine * cosine * r0 + cosine * sa * cross + sa * sa * row(t, 3)
        v_da = cosine * cosine * sum1_vda + cosine * sa * row(t, 4) + sa * sa * row(t, 5)
        v_dv = cosine * cosine * sum1_vdv + 2.0 * cosine * sa * row(t, 6) + sa * sa * row(t, 7)
        along1 = v_da - r1 * v_dv
        ritz[0:1, :] = value0
        cs, ss, r1s, l1s = scalar(cosine), scalar(sa), scalar(r1), scalar(along1)
        finish(2, xq_buf)

        def build(s, carry):
            for e in range(ENV):
                di = dcol_of(s, e)
                v = xs_buf[s, e].astype(F32) * c0s
                da = xd_buf[s, e].astype(F32)
                q = xq_buf[s, e].astype(F32)
                corr = da - v * (r0s * di + along0s)
                v1 = cs * v + ss * corr
                c1 = cs * da + ss * (q * di) - v1 * (r1s * di + l1s)
                xt_buf[s, e] = c1.astype(BF)
            return carry

        lax.fori_loop(0, wide, build, 0)

        def own_step(s, carry):
            a, v, q, corr, di = va[s], start[s], vq[s], vc[s], dinv[s]
            v1 = cs * v + ss * corr
            a1 = cs * a + ss * q
            c1 = (a1 - r1s * v1) * di - l1s * v1
            start[s] = v1
            vc[s] = c1
            return (carry[0] + fold(c1 * c1), carry[1] + fold(c1 * a1))

        pre = over_sectors(own_step, zeros(2))

        def done2(s, acc, carry):
            q = acc * live[s]
            return (carry[0] + fold(start[s] * q), carry[1] + fold(vc[s] * q))

        post = over_sectors(apply(xt_buf, done2), zeros(2))
        sum_begin(3, list(pre) + list(post))
        for e, buf in ((0, xs_buf), (1, xd_buf), (2, xq_buf)):
            drain(e, buf)
        for c in d_copies():
            c.wait_send()

        @pl.when(has_out)
        def _():
            for c in d_outer():
                c.wait_send()

        sum_middle(3)
        for r in range(3):
            sum_drain(r)
        t = sum_end(3)
        alpha = lax.rsqrt(row(t, 0) + 1e-06)
        coupling = 0.5 * alpha * (row(t, 1) + row(t, 2))
        upper = alpha * alpha * row(t, 3)
        cosine, sine, value1 = rotation(r1, upper, coupling)
        ritz[1:2, :] = value1
        cs2, ss2 = scalar(cosine), scalar(sine * alpha)
        for s in range(sectors):
            out[s] = cs2 * start[s] + ss2 * vc[s]
        sum_drain(3)

    return kernel, near, zs, wide


def local(wavefunction, left_env, right_env, shifts, block_dims, precond):
    sectors, rows, cols = wavefunction.shape
    terms = left_env.shape[1]
    nsec = lax.axis_size("sec")
    kernel, near, zs, wide = make_kernel(nsec, sectors, terms, rows, cols)
    vmem = pl.BlockSpec(memory_space=pltpu.VMEM)
    smem = pl.BlockSpec(memory_space=pltpu.SMEM)
    hbm = pl.BlockSpec(memory_space=pl.ANY)
    held = pltpu.VMEM((wide, ENV, rows, cols), BF)
    field = pltpu.VMEM((sectors, rows, cols), F32)
    dma = pltpu.SemaphoreType.DMA
    vector, ritz = pl.pallas_call(
        kernel,
        out_shape=(
            jax.ShapeDtypeStruct((sectors, rows, cols), F32),
            jax.ShapeDtypeStruct((2, LANES), F32),
        ),
        in_specs=[smem, smem, vmem, vmem, hbm, hbm],
        out_specs=(vmem, vmem),
        scratch_shapes=[
            pltpu.VMEM(left_env.shape, BF),
            pltpu.VMEM(right_env.shape, BF),
            held, held, held, held,
            pltpu.VMEM((wide, ENV, 1, LANES), F32),
            pltpu.VMEM((LANES, LANES), F32),
            pltpu.VMEM((LANES, LANES), F32),
            field, field, field, field, field, field, field, field,
            pltpu.VMEM((4, near, 8, LANES), F32),
            pltpu.VMEM((4, zs, 8, LANES), F32),
            pltpu.VMEM((8, LANES), F32),
            dma((2,)),
            dma((3, ENV)), dma((3, ENV)), dma((3, ENV)), dma((3, ENV)),
            dma((3, 4, ENV)),
            dma((3, ENV)), dma((3, ENV)),
            dma((4,)), dma((4,)), dma((4,)), dma((4,)),
        ],
        compiler_params=pltpu.CompilerParams(
            collective_id=0, has_side_effects=True, vmem_limit_bytes=48 << 20
        ),
    )(shifts, block_dims, wavefunction, precond, left_env, right_env)
    return vector, ritz[:, 0]


def solution(mesh):
    in_specs = (
        P("sec", "env", None),
        P("sec", None, "env", None),
        P("sec", None, None, None),
        P(),
        P("sec", None),
        P("sec", "env"),
    )
    out_specs = (P("sec", "env", None), P())
    return jax.shard_map(local, mesh=mesh, in_specs=in_specs, out_specs=out_specs, check_vma=False)
```

time: 906 us -> 82.4 us (0.09)
  blocking collectives: 708 us -> 0 us
  matrix products: 94.9 us -> 0 us
  Pallas kernels: 0 us -> 75.6 us
  between operations: 44.1 us -> 0.64 us
  starting transfers between devices: 23.8 us -> 0 us
  other arithmetic: 16.1 us -> 0 us
    psum x9 -> x0, blocking collectives: 676 us -> none  [the longest x2 154 us: local(): lax.psum((local_product(unit, applied), local_product(vector, applied_uni...]
    dot_general x48 -> x0, matrix products: 94.9 us -> none  [apply_hamiltonian(): jnp.einsum('sij,sjk->sik', partial_rows, right_env[:, term_no], preferred...]
    pallas_call x0 -> x1, Pallas kernels: none -> 75.6 us  [local(): pl.pallas_call(kernel, out_shape=(jax.ShapeDtypeStruct((sectors, rows, co...]
    all_gather x3 -> x0, blocking collectives: 32.4 us -> none  [apply_hamiltonian(): whole = lax.all_gather(narrow, 'env', axis=1, tiled=True)]
    ppermute x6 -> x0, starting transfers between devices: 23.8 us -> none  [the longest x3 18.1 us: padded(): lax.ppermute(lax.slice_in_dim(block, block.shape[dim] - width, None, axis...]
    reduce_sum x6 -> x0, other arithmetic: 12.6 us -> none  [local_product(): return jnp.sum(first * second) / count]
  transfers between devices with their start and end apart: 6 -> 0, of which waited for: 2 -> 0; matrix products, arithmetic and copies ran while one was open for 1% -> 0% of each run, Pallas kernels for 0% -> 0%
where the time goes in v1:
time: 82.4 us; the launch traced here: 82.2 us
  Pallas kernels  75.6 us (92%)
  local copies, waits for them, and re-layouts  5.97 us (7%)
    pallas_call x1, Pallas kernels, local(): pl.pallas_call(kernel, out_shape=(jax.ShapeDtypeStruct((sectors, rows, co...  75.6 us
    unnamed x10, local copies, waits for them, and re-layouts  5.34 us

profile of v1, /device:TPU:1, one launch (start us, length us, event | category | flops | bytes accessed | tf_op | source)
XLA Modules:
  0.0 82.2 jit_solution(7531134325670951595)
XLA Ops:
  0.6 0.8 copy.9.dims
  1.4 0.0 copy-start
  1.4 1.6 %copy-done = bf16[4,16,64,256]{3,2,1,0:T(8,128)(2,1)S(1)} copy-done((bf16[4,16,64,256]{3,2,1,0:T(8,128)(2,1)S(1)}, bf16[4,16,64,256]{3,2,1,0:T(8,128)(2,1)}, u32[]{:S(2)}) %copy-start) | copy-done | bytes 2097176
  3.0 0.0 copy-start.1
  3.0 0.9 %copy-done.1 = f32[4,64,256]{2,1,0:T(8,128)S(1)} copy-done((f32[4,64,256]{2,1,0:T(8,128)S(1)}, f32[4,64,256]{2,1,0:T(8,128)}, u32[]{:S(2)}) %copy-start.1) | copy-done | bytes 262168
  3.9 0.0 copy-start.2
  3.9 0.7 copy-done.2
  4.6 0.0 copy-start.3
  4.6 0.7 copy-done.3
  5.3 75.6 %shard_map.77 = (f32[4,64,256]{2,1,0:T(8,128)S(1)}, f32[2,128]{1,0:T(2,128)S(1)}) custom-call(s32[16]{0:T(128)S(1)} %copy-done.3, s32[4,2]{1,0:T(4,128)S(1)} %copy.9.dims, f32[4,64,256]{2,1,0:T(8,128)S(1)} %copy-done.1, f32[4,64]{1,0:T(4,128)S(1)} %copy-done.2, bf16[4,16,64,256]{3,2,1,0:T(8,128)(2,1)S(1)} %copy-done, bf16[4,16,256,256]{3,2,1,0:T(8,128)(2,1)} %right_hbm.1), custom_call_target="tpu_custom_call" | custom-call | tf_op jit(solution)/shard_map/pallas_call | solution.py:472
  80.8 0.6 slice_reduce_fusion
  81.5 0.7 copy.11
Async XLA Ops:
  1.4 1.6 %copy-start = (bf16[4,16,64,256]{3,2,1,0:T(8,128)(2,1)S(1)}, bf16[4,16,64,256]{3,2,1,0:T(8,128)(2,1)}, u32[]{:S(2)}) copy-start(bf16[4,16,64,256]{3,2,1,0:T(8,128)(2,1)} %left_hbm.1) | copy-start | bytes 6291460
  3.0 0.9 %copy-start.1 = (f32[4,64,256]{2,1,0:T(8,128)S(1)}, f32[4,64,256]{2,1,0:T(8,128)}, u32[]{:S(2)}) copy-start(f32[4,64,256]{2,1,0:T(8,128)} %wf.1) | copy-start | bytes 786436
  3.9 0.7 copy-start.2
  4.6 0.7 copy-start.3

commit v2 on v1

v2 whole, which is shorter than its diff:
```python
import jax
import jax.numpy as jnp
from jax import lax
from jax.experimental import pallas as pl
from jax.experimental.pallas import tpu as pltpu
from jax.sharding import PartitionSpec as P

MAXSHIFT = 2
BF = jnp.bfloat16
F32 = jnp.float32
MESH = pl.DeviceIdType.MESH
ENV = 4
LANES = 128
ZS = 8
ORDER = (1, 3, 2)


def dot(a, b):
    return jnp.dot(a, b, preferred_element_type=F32)


def make_kernel(nsec, sectors, terms, rows, cols):
    zs = ZS
    xs = nsec // (2 * zs)
    near = 2 * ENV * xs
    wide = sectors + 2 * MAXSHIFT
    half = cols // 2
    count = float(nsec * sectors * ENV * rows * cols)
    halves = (0, 1)

    def kernel(
        shifts_hbm, dims_hbm, wf_hbm, prec_hbm, left_hbm, right_hbm, out, ritz,
        shifts, dims, wf, prec, left, right,
        xs0, xs1, xd0, xd1, xq0, xq1, xt0, xt1, dall, dpad, dcols, dinv,
        live, start, va, vb, vh, vq, vc, vg, tmp, near_slots, far_slots,
        load_sem, go_sem, gi_sem, out_sem, in_sem, send_sem, d_send, d_recv,
        near_send, near_recv, far_send, far_recv, ready,
    ):
        fields = ((xs0, xs1), (xd0, xd1), (xq0, xq1))
        sec = lax.axis_index("sec")
        y = lax.axis_index("env")
        core = lax.rem(sec, 2)
        chip = sec // 2
        z = lax.rem(chip, zs)
        x = chip // zs
        has_out = jnp.logical_or(
            jnp.logical_and(core == 0, sec > 0), jnp.logical_and(core == 1, sec < nsec - 1)
        )
        outer = jnp.clip(sec + 2 * core - 1, 0, nsec - 1)
        inner = sec + 1 - 2 * core
        out_src, out_dst = 2 * core, 6 * (1 - core)
        in_src, in_dst = 2 * (1 - core), 6 * core

        def yy(k):
            return lax.rem(y + k + ENV, ENV)

        near_rank = (core * ENV + y) * xs + x

        def near_peer(k):
            m = lax.rem(near_rank + k, near)
            return (((lax.rem(m, xs) * zs + z) * 2 + m // (xs * ENV)), lax.rem(m // xs, ENV))

        def far_peer(k):
            m = lax.rem(z + k + zs, zs)
            return (((x * zs + m) * 2 + core), y)

        def x_peer(k):
            return ((lax.rem(x + k, xs) * zs + z) * 2 + core, y)

        greeted = [(sec, yy(k)) for k in range(1, ENV)] + [(inner, yy(k)) for k in range(ENV)]
        greeted += [x_peer(k) for k in range(1, xs)] + [far_peer(1), far_peer(-1)]

        loads = [
            pltpu.make_async_copy(a, b, load_sem.at[i])
            for i, (a, b) in enumerate((
                (wf_hbm, wf), (dims_hbm, dims), (prec_hbm, prec), (shifts_hbm, shifts), (left_hbm, left), (right_hbm, right),
            ))
        ]
        for load in loads:
            load.start()

        zero = jnp.zeros((MAXSHIFT, ENV, rows, half), BF)
        ones = jnp.ones((MAXSHIFT, ENV, 1, LANES), F32)

        @pl.when(sec == 0)
        def _():
            for pair in fields:
                for buf in pair:
                    buf[0:MAXSHIFT] = zero
            dall[0:MAXSHIFT] = ones

        @pl.when(sec == nsec - 1)
        def _():
            for pair in fields:
                for buf in pair:
                    buf[wide - MAXSHIFT : wide] = zero
            dall[wide - MAXSHIFT : wide] = ones

        def greet(semaphore):
            for peer in greeted:
                pl.semaphore_signal(semaphore, inc=1, device_id=peer, device_id_type=MESH)

            @pl.when(has_out)
            def _():
                pl.semaphore_signal(semaphore, inc=1, device_id=(outer, y), device_id_type=MESH)

        barrier = pltpu.get_barrier_semaphore()
        greet(barrier)
        expected = len(greeted) + jnp.where(has_out, 1, 0)

        for load in loads[:3]:
            load.wait()

        def put(pair, s, value):
            for h in halves:
                pair[h][MAXSHIFT + s, y] = value[:, h * half : (h + 1) * half].astype(BF)

        def fold(v, op=jnp.add):
            parts = [
                v[r * 8 : r * 8 + 8, c * LANES : (c + 1) * LANES]
                for r in range(rows // 8)
                for c in range(cols // LANES)
            ]
            while len(parts) > 1:
                parts = [op(a, b) for a, b in zip(parts[::2], parts[1::2], strict=True)]
            return parts[0]

        row_ids = y * rows + lax.broadcasted_iota(jnp.int32, (rows, cols), 0)
        col_ids = lax.broadcasted_iota(jnp.int32, (rows, cols), 1)
        largest = jnp.zeros((8, LANES), F32)
        for s in range(sectors):
            ok = jnp.logical_and(row_ids < dims[0, s], col_ids < dims[1, s])
            mask = jnp.where(ok, 1.0, 0.0).astype(F32)
            live[s] = mask
            st = wf[s] * mask
            start[s] = st
            put(fields[0], s, st)
            largest = jnp.maximum(largest, fold(jnp.abs(st), jnp.maximum))
            dall[MAXSHIFT + s, y, :, 0:rows] = prec[s : s + 1, :]
        dpad[...] = jnp.ones((LANES, LANES), F32)
        dpad[0:sectors, 0:rows] = prec[...]
        columns = 1.0 / jnp.transpose(dpad[...])
        for s in range(sectors):
            dinv[s] = jnp.broadcast_to(columns[0:rows, s : s + 1], (rows, LANES))
        peak = jnp.max(jnp.max(largest, axis=0, keepdims=True), axis=1, keepdims=True)
        peak = jnp.broadcast_to(jnp.where(peak > 0.0, peak, 1.0), (1, LANES))

        def across(r):
            return jnp.concatenate([r] * (cols // LANES), axis=1)

        def inverse(s):
            return jnp.concatenate([dinv[s]] * (cols // LANES), axis=1)

        pl.semaphore_wait(barrier, expected)

        def cp(src, dst, ss, rs, dev):
            return pltpu.make_async_remote_copy(
                src_ref=src, dst_ref=dst, send_sem=ss, recv_sem=rs, device_id=dev, device_id_type=MESH
            )

        def gather_outer(e, h, k):
            part = fields[e][h].at[pl.ds(MAXSHIFT + out_src, 2), y]
            return cp(part, part, send_sem.at[e, h, 0, k], go_sem.at[e, h, k], (sec, yy(k)))

        def gather_inner(e, h, k):
            part = fields[e][h].at[pl.ds(MAXSHIFT + in_src, 2), y]
            return cp(part, part, send_sem.at[e, h, 1, k], gi_sem.at[e, h, k], (sec, yy(k)))

        def relay_outer(e, h, k):
            src = fields[e][h].at[pl.ds(MAXSHIFT + out_src, 2), yy(-k)]
            dst = fields[e][h].at[pl.ds(out_dst, 2), yy(-k)]
            return cp(src, dst, send_sem.at[e, h, 2, k], out_sem.at[e, h, k], (outer, y))

        def relay_inner(e, h, k):
            src = fields[e][h].at[pl.ds(MAXSHIFT + in_src, 2), yy(-k)]
            dst = fields[e][h].at[pl.ds(in_dst, 2), yy(-k)]
            return cp(src, dst, send_sem.at[e, h, 3, k], in_sem.at[e, h, k], (inner, y))

        def begin(e):
            for h in halves:
                for k in ORDER:
                    gather_outer(e, h, k).start()

            @pl.when(has_out)
            def _():
                for h in halves:
                    relay_outer(e, h, 0).start()

            for h in halves:
                for k in ORDER:
                    gather_inner(e, h, k).start()
            for h in halves:
                relay_inner(e, h, 0).start()

        def pass_outer(e):
            for h in halves:
                for k in ORDER:
                    gather_outer(e, h, k).wait_recv()

                    @pl.when(has_out)
                    def _():
                        relay_outer(e, h, k).start()

        def pass_inner(e):
            for h in halves:
                for k in ORDER:
                    gather_inner(e, h, k).wait_recv()
                    relay_inner(e, h, k).start()

        def finish(e, h):
            @pl.when(has_out)
            def _():
                for k in (0,) + ORDER:
                    relay_outer(e, h, k).wait_recv()

            for k in (0,) + ORDER:
                relay_inner(e, h, k).wait_recv()

        def drain(e):
            for h in halves:
                for k in ORDER:
                    gather_outer(e, h, k).wait_send()
                    gather_inner(e, h, k).wait_send()
                for k in (0,) + ORDER:
                    relay_inner(e, h, k).wait_send()

                @pl.when(has_out)
                def _():
                    for k in (0,) + ORDER:
                        relay_outer(e, h, k).wait_send()

        def near_copy(r, k):
            ref = near_slots.at[r, near_rank]
            return cp(ref, ref, near_send.at[r], near_recv.at[r], near_peer(k))

        def far_copy(r, k):
            ref = far_slots.at[r, z]
            return cp(ref, ref, far_send.at[r], far_recv.at[r], far_peer(k))

        def near_all(r):
            ref = near_slots.at[r, pl.ds(0, near - 1)]
            return cp(ref, ref, near_send.at[r], near_recv.at[r], near_peer(1))

        def far_all(r):
            ref = far_slots.at[r, pl.ds(0, zs - 1)]
            return cp(ref, ref, far_send.at[r], far_recv.at[r], far_peer(1))

        def sum_begin(r, parts, last=None):
            parts = [jnp.sum(p, axis=0, keepdims=True) for p in parts]
            parts = parts + [jnp.zeros((1, LANES), F32)] * (8 - len(parts))
            if last is not None:
                parts[7] = last
            near_slots[r, near_rank] = jnp.concatenate(parts, axis=0)
            for k in range(1, near):
                near_copy(r, k).start()

        def total_of(slots, scaled):
            t = slots
            if not scaled:
                return jnp.sum(t, axis=0)
            scale = t[:, 7:8, :]
            top = jnp.max(scale, axis=0, keepdims=True)
            ratio = scale / top
            t = jnp.sum(t * (ratio * ratio), axis=0)
            keep = lax.broadcasted_iota(jnp.int32, (8, LANES), 0) == 7
            return jnp.where(keep, jnp.broadcast_to(top[0], (8, LANES)), t)

        def sum_middle(r, scaled=False):
            near_all(r).wait_recv()
            far_slots[r, z] = total_of(near_slots[r], scaled)
            for k in range(1, zs):
                far_copy(r, k).start()

        def sum_end(r, scaled=False):
            far_all(r).wait_recv()
            t = total_of(far_slots[r], scaled)
            m = jnp.sum(t, axis=1, keepdims=True) * (1.0 / count)
            return jnp.broadcast_to(m, (8, LANES)), t[7:8, :]

        def sum_drain(r):
            near_all(r).wait_send()
            far_all(r).wait_send()

        def row(t, i):
            return t[i : i + 1, :]

        def h_half(pair, h, s):
            acc = jnp.zeros((rows, cols), F32)
            for w in range(terms):
                source = pair[h][s + MAXSHIFT + shifts[w]].reshape(ENV * rows, half)
                part = dot(left[s, w], source).astype(BF)
                acc = acc + dot(part, right[s, w, h * half : (h + 1) * half, :])
            return acc

        def apply_arriving(e, done):
            finish(e, 0)
            for s in range(sectors):
                tmp[s] = h_half(fields[e], 0, s)
            finish(e, 1)
            for s in range(sectors):
                done(s, (tmp[s] + h_half(fields[e], 1, s)) * live[s])

        def apply_built(dst):
            for s in range(sectors):
                dst[s] = h_half((xt0, xt1), 0, s)
            for s in range(sectors):
                dst[s] = (dst[s] + h_half((xt0, xt1), 1, s)) * live[s]

        begin(0)
        greet(ready.at[0])

        def d_copies():
            piece = dall.at[pl.ds(MAXSHIFT, sectors), y]
            res = [cp(piece, piece, d_send.at[0, k], d_recv.at[0, k], (sec, yy(k))) for k in range(1, ENV)]
            for k in range(ENV):
                src = dall.at[pl.ds(MAXSHIFT + in_src, 2), y]
                dst = dall.at[pl.ds(in_dst, 2), y]
                res.append(cp(src, dst, d_send.at[1, k], d_recv.at[1, k], (inner, yy(k))))
            return res

        def d_outer():
            res = []
            for k in range(ENV):
                src = dall.at[pl.ds(MAXSHIFT + out_src, 2), y]
                dst = dall.at[pl.ds(out_dst, 2), y]
                res.append(cp(src, dst, d_send.at[2, k], d_recv.at[2, k], (outer, yy(k))))
            return res

        for c in d_copies():
            c.start()
        pl.semaphore_wait(ready.at[0], expected)
        for k in (2, -2):
            pl.semaphore_signal(ready.at[1], inc=1, device_id=far_peer(k), device_id_type=MESH)

        @pl.when(has_out)
        def _():
            for c in d_outer():
                c.start()

        pass_outer(0)
        pass_inner(0)
        for load in loads[3:]:
            load.wait()
        inv_peak = across(1.0 / peak)
        sums = [jnp.zeros((8, LANES), F32) for _ in range(4)]

        def done0(s, a):
            di = inverse(s)
            da = a * di
            va[s] = a
            put(fields[1], s, da)
            u = start[s] * inv_peak
            ua = a * inv_peak
            for i, n in enumerate((u * u, u * ua, u * (ua * di), u * (u * di))):
                sums[i] = sums[i] + fold(n)

        apply_arriving(0, done0)

        pl.semaphore_wait(ready.at[1], 2)
        sum_begin(1, sums, peak)
        begin(1)
        for c in d_copies():
            c.wait_recv()

        @pl.when(has_out)
        def _():
            for c in d_outer():
                c.wait_recv()

        for s in range(wide):
            for e in range(ENV):
                dpad[s * ENV + e : s * ENV + e + 1, 0:rows] = dall[s, e, :, 0:rows]
        columns = 1.0 / jnp.transpose(dpad[...])
        for s in range(wide):
            for e in range(ENV):
                k = s * ENV + e
                dcols[s, e] = jnp.broadcast_to(columns[0:rows, k : k + 1], (rows, LANES))

        def scale_start(s, carry):
            for h in halves:
                for e in range(ENV):
                    (xt0, xt1)[h][s, e] = (fields[0][h][s, e].astype(F32) * dcols[s, e]).astype(BF)
            return carry

        lax.fori_loop(0, wide, scale_start, 0)
        apply_built(vh)
        pass_outer(1)
        sum_middle(1, True)
        pass_inner(1)

        def done1(s, b):
            vb[s] = b

        apply_arriving(1, done1)
        t, top = sum_end(1, True)
        c0 = lax.rsqrt(top * (top * row(t, 0)) + 1e-06)
        k2 = (c0 * top) * (c0 * top)
        r0, v_da0, v_dv0 = k2 * row(t, 1), k2 * row(t, 2), k2 * row(t, 3)
        along0 = v_da0 - r0 * v_dv0
        c0w, r0w, l0w = across(c0), across(r0), across(along0)
        sums = [jnp.zeros((8, LANES), F32) for _ in range(8)]
        for s in range(sectors):
            di = inverse(s)
            v, a, hd, b = start[s] * c0w, va[s] * c0w, vh[s] * c0w, vb[s] * c0w
            da = a * di
            q = b - r0w * hd - l0w * a
            corr = da - r0w * (v * di) - l0w * v
            dq, dc = q * di, corr * di
            put(fields[2], s, dq)
            start[s], va[s], vh[s], vb[s], vq[s], vc[s] = v, a, hd, b, q, corr
            new = (
                corr * corr, corr * a, v * q, corr * q,
                v * dq + corr * da, corr * dq, v * dc, corr * dc,
            )
            sums = [c + fold(n) for c, n in zip(sums, new, strict=True)]

        sum_begin(2, sums)
        begin(2)

        def build(s, carry):
            for e in range(ENV):
                di = dcols[s, e]
                for_da = c0 * di
                for_s = -for_da * (r0 * di + along0)
                for h in halves:
                    da = fields[1][h][s, e].astype(F32)
                    st = fields[0][h][s, e].astype(F32)
                    (xt0, xt1)[h][s, e] = (for_da * da + for_s * st).astype(BF)
            return carry

        lax.fori_loop(0, wide, build, 0)
        apply_built(vg)
        pass_outer(2)
        sum_middle(2)
        pass_inner(2)

        def done2(s, n):
            tmp[s] = n

        apply_arriving(2, done2)
        t, _ = sum_end(2)

        def rotation(rayleigh, upper, coupling):
            px, py = upper - rayleigh, -2.0 * coupling
            big = jnp.maximum(jnp.abs(px), jnp.abs(py))
            some = big > 0.0
            safe = jnp.where(some, big, 1.0)
            ux, uy = jnp.where(some, px / safe, 1.0), py / safe
            h = jnp.sqrt(ux * ux + uy * uy)
            large = jnp.sqrt(0.5 * (1.0 + jnp.abs(ux) / h))
            small = jnp.abs(uy) / (2.0 * h * large)
            cosine = jnp.where(ux >= 0.0, large, small)
            sine = jnp.where(ux >= 0.0, small, large)
            sine = jnp.where(uy > 0.0, sine, -sine)
            mid = 0.5 * (rayleigh - upper)
            return cosine, sine, 0.5 * (rayleigh + upper) - jnp.sqrt(mid * mid + coupling * coupling)

        alpha = lax.rsqrt(row(t, 0) + 1e-06)
        cross = row(t, 1) + row(t, 2)
        cosine, sine, value0 = rotation(r0, alpha * alpha * row(t, 3), 0.5 * alpha * cross)
        sa = sine * alpha
        r1 = cosine * cosine * r0 + cosine * sa * cross + sa * sa * row(t, 3)
        v_da = cosine * cosine * v_da0 + cosine * sa * row(t, 4) + sa * sa * row(t, 5)
        v_dv = cosine * cosine * v_dv0 + 2.0 * cosine * sa * row(t, 6) + sa * sa * row(t, 7)
        along1 = v_da - r1 * v_dv
        ritz[0:1, :] = value0
        cw, sw, r1w, l1w = across(cosine), across(sa), across(r1), across(along1)
        sums = [jnp.zeros((8, LANES), F32) for _ in range(4)]
        for s in range(sectors):
            di = inverse(s)
            v1 = cw * start[s] + sw * vc[s]
            a1 = cw * va[s] + sw * vq[s]
            c1 = (a1 - r1w * v1) * di - l1w * v1
            q1 = cw * vb[s] + sw * tmp[s] - r1w * (cw * vh[s] + sw * vg[s]) - l1w * a1
            start[s] = v1
            vc[s] = c1
            sums = [c + fold(n) for c, n in zip(sums, (c1 * c1, c1 * a1, v1 * q1, c1 * q1), strict=True)]
        sum_begin(0, sums)
        for e in range(3):
            drain(e)
        for c in d_copies():
            c.wait_send()

        @pl.when(has_out)
        def _():
            for c in d_outer():
                c.wait_send()

        sum_middle(0)
        for r in (1, 2):
            sum_drain(r)
        t, _ = sum_end(0)
        alpha = lax.rsqrt(row(t, 0) + 1e-06)
        coupling = 0.5 * alpha * (row(t, 1) + row(t, 2))
        cosine, sine, value1 = rotation(r1, alpha * alpha * row(t, 3), coupling)
        ritz[1:2, :] = value1
        cw, sw = across(cosine), across(sine * alpha)
        for s in range(sectors):
            out[s] = cw * start[s] + sw * vc[s]
        sum_drain(0)

    return kernel, near, zs, wide, half


def local(wavefunction, left_env, right_env, shifts, block_dims, precond):
    sectors, rows, cols = wavefunction.shape
    terms = left_env.shape[1]
    nsec = lax.axis_size("sec")
    kernel, near, zs, wide, half = make_kernel(nsec, sectors, terms, rows, cols)
    vmem = pl.BlockSpec(memory_space=pltpu.VMEM)
    hbm = pl.BlockSpec(memory_space=pltpu.HBM)
    held = pltpu.VMEM((wide, ENV, rows, half), BF)
    field = pltpu.VMEM((sectors, rows, cols), F32)
    dma = pltpu.SemaphoreType.DMA
    vector, ritz = pl.pallas_call(
        kernel,
        out_shape=(
            jax.ShapeDtypeStruct((sectors, rows, cols), F32),
            jax.ShapeDtypeStruct((2, LANES), F32),
        ),
        in_specs=[hbm] * 6,
        out_specs=(vmem, vmem),
        scratch_shapes=[
            pltpu.SMEM(shifts.shape, jnp.int32),
            pltpu.SMEM((2, sectors), jnp.int32),
            pltpu.VMEM(wavefunction.shape, F32),
            pltpu.VMEM(precond.shape, F32),
            pltpu.VMEM(left_env.shape, BF),
            pltpu.VMEM(right_env.shape, BF),
            held, held, held, held, held, held, held, held,
            pltpu.VMEM((wide, ENV, 1, LANES), F32),
            pltpu.VMEM((LANES, LANES), F32),
            pltpu.VMEM((wide, ENV, rows, LANES), F32),
            pltpu.VMEM((sectors, rows, LANES), F32),
            field, field, field, field, field, field, field, field, field,
            pltpu.VMEM((3, near, 8, LANES), F32),
            pltpu.VMEM((3, zs, 8, LANES), F32),
            dma((6,)),
            dma((3, 2, ENV)), dma((3, 2, ENV)), dma((3, 2, ENV)), dma((3, 2, ENV)),
            dma((3, 2, 4, ENV)),
            dma((3, ENV)), dma((3, ENV)),
            dma((3,)), dma((3,)), dma((3,)), dma((3,)),
            pltpu.SemaphoreType.REGULAR((2,)),
        ],
        compiler_params=pltpu.CompilerParams(
            collective_id=0, has_side_effects=True, vmem_limit_bytes=56 << 20
        ),
    )(shifts, block_dims.T, wavefunction, precond, left_env, right_env)
    return vector, ritz[:, 0]


def solution(mesh):
    in_specs = (
        P("sec", "env", None),
        P("sec", None, "env", None),
        P("sec", None, None, None),
        P(),
        P("sec", None),
        P("sec", "env"),
    )
    out_specs = (P("sec", "env", None), P())
    return jax.shard_map(local, mesh=mesh, in_specs=in_specs, out_specs=out_specs, check_vma=False)
```

time: 82.4 us -> 62.2 us (0.75)
  Pallas kernels: 75.6 us -> 58.5 us
  local copies, waits for them, and re-layouts: 5.97 us -> 2.96 us
    pallas_call x1, Pallas kernels: 75.6 us -> 58.5 us  [local(): pl.pallas_call(kernel, out_shape=(jax.ShapeDtypeStruct((sectors, rows, co...]
    unnamed x10 -> x1, local copies, waits for them, and re-layouts: 5.34 us -> 1.67 us
where the time goes in v2:
time: 62.2 us; the launch traced here: 62.1 us
  Pallas kernels  58.5 us (94%)
  local copies, waits for them, and re-layouts  2.96 us (5%)
  between operations  0.64 us (1%)
    pallas_call x1, Pallas kernels, local(): pl.pallas_call(kernel, out_shape=(jax.ShapeDtypeStruct((sectors, rows, co...  58.5 us
    unnamed x1, local copies, waits for them, and re-layouts  1.67 us
    slice x1, local copies, waits for them, and re-layouts, local(): return (vector, ritz[:, 0])  1.29 us

profile of v2, /device:TPU:1, one launch (start us, length us, event | category | flops | bytes accessed | tf_op | source)
XLA Modules:
  0.0 62.1 jit_solution(18393119152125864840)
XLA Ops:
  0.6 58.5 %shard_map.77 = (f32[4,64,256]{2,1,0:T(8,128)}, f32[2,128]{1,0:T(2,128)}) custom-call(s32[16]{0:T(128)} %shifts_hbm.1, s32[2,4]{1,0:T(2,128)} %bitcast.1, f32[4,64,256]{2,1,0:T(8,128)} %wf_hbm.1, f32[4,64]{1,0:T(4,128)} %prec_hbm.1, bf16[4,16,64,256]{3,2,1,0:T(8,128)(2,1)} %left_hbm.1, bf16[4,16,256,256]{3,2,1,0:T(8,128)(2,1)} %right_hbm.1), custom_call_target="tpu_custom_call" | custom-call | tf_op jit(solution)/shard_map/pallas_call | solution.py:515
  59.1 1.3 %slice_reduce_fusion = f32[2]{0:T(128)} fusion(f32[2,128]{1,0:T(2,128)} %get-tuple-element.5), kind=kLoop, calls=%fused_computation | loop fusion | bytes 16 | tf_op jit(solution)/shard_map/slice | solution.py:549
  60.4 1.7 %copy.9 = f32[4,64,256]{2,1,0:T(8,128)} copy(f32[4,64,256]{2,1,0:T(8,128)} %get-tuple-element.8) | data formatting | bytes 524288

commit v3 on v2

--- a/solution.py
+++ b/solution.py
@@ -543,9 +543,9 @@
             pltpu.SemaphoreType.REGULAR((2,)),
         ],
         compiler_params=pltpu.CompilerParams(
-            collective_id=0, has_side_effects=True, vmem_limit_bytes=56 << 20
+            collective_id=0, has_side_effects=True, vmem_limit_bytes=40 << 20
         ),
-    )(shifts, block_dims.T, wavefunction, precond, left_env, right_env)
+    )(*(pltpu.with_memory_space_constraint(a, pltpu.HBM) for a in (shifts, block_dims.T, wavefunction, precond, left_env, right_env)))
     return vector, ritz[:, 0]
 
 

time: 62.2 us -> 59.9 us (0.963)
  local copies, waits for them, and re-layouts: 2.96 us -> 1.33 us
  Pallas kernels: 58.5 us -> 57.8 us
    unnamed x1, local copies, waits for them, and re-layouts: 1.67 us -> 0.7 us
    pallas_call x1, Pallas kernels: 58.5 us -> 57.8 us  [local(): pl.pallas_call(kernel, out_shape=(jax.ShapeDtypeStruct((sectors, rows, co...]
    slice x1, local copies, waits for them, and re-layouts: 1.29 us -> 0.63 us  [local(): return (vector, ritz[:, 0])]
where the time goes in v3:
time: 59.9 us; the launch traced here: 59.8 us
  Pallas kernels  57.8 us (96%)
  local copies, waits for them, and re-layouts  1.33 us (2%)
  between operations  0.64 us (1%)
    pallas_call x1, Pallas kernels, local(): pl.pallas_call(kernel, out_shape=(jax.ShapeDtypeStruct((sectors, rows, co...  57.8 us

profile of v3, /device:TPU:1, one launch (start us, length us, event | category | flops | bytes accessed | tf_op | source)
XLA Modules:
  0.0 59.8 jit_solution(5616439277668857589)
XLA Ops:
  0.6 57.8 %shard_map.77 = (f32[4,64,256]{2,1,0:T(8,128)S(1)}, f32[2,128]{1,0:T(2,128)S(1)}) custom-call(s32[16]{0:T(128)} %shifts_hbm.1, s32[2,4]{1,0:T(2,128)} %bitcast.1, f32[4,64,256]{2,1,0:T(8,128)} %wf_hbm.1, f32[4,64]{1,0:T(4,128)} %prec_hbm.1, bf16[4,16,64,256]{3,2,1,0:T(8,128)(2,1)} %left_hbm.1, bf16[4,16,256,256]{3,2,1,0:T(8,128)(2,1)} %right_hbm.1), custom_call_target="tpu_custom_call" | custom-call | tf_op jit(solution)/shard_map/pallas_call | solution.py:515
  58.4 0.6 %slice_reduce_fusion = f32[2]{0:T(128)} fusion(f32[2,128]{1,0:T(2,128)S(1)} %get-tuple-element.5), kind=kLoop, calls=%fused_computation | loop fusion | bytes 16 | tf_op jit(solution)/shard_map/slice | solution.py:549
  59.1 0.7 %copy.9 = f32[4,64,256]{2,1,0:T(8,128)} copy(f32[4,64,256]{2,1,0:T(8,128)S(1)} %get-tuple-element.8) | data formatting | bytes 524288

commit v4 on v3

--- a/solution.py
+++ b/solution.py
@@ -176,10 +176,11 @@
             dst = fields[e][h].at[pl.ds(in_dst, 2), yy(-k)]
             return cp(src, dst, send_sem.at[e, h, 3, k], in_sem.at[e, h, k], (inner, y))
 
-        def begin(e):
+        def begin(e, between=lambda: None):
             for h in halves:
                 for k in ORDER:
                     gather_outer(e, h, k).start()
+            between()
 
             @pl.when(has_out)
             def _():
@@ -245,25 +246,29 @@
             ref = far_slots.at[r, pl.ds(0, zs - 1)]
             return cp(ref, ref, far_send.at[r], far_recv.at[r], far_peer(1))
 
+        lane = lax.broadcasted_iota(jnp.int32, (1, LANES), 1)
+        diagonal = lax.broadcasted_iota(jnp.int32, (8, LANES), 0) == lax.broadcasted_iota(jnp.int32, (8, LANES), 1)
+
         def sum_begin(r, parts, last=None):
             parts = [jnp.sum(p, axis=0, keepdims=True) for p in parts]
             parts = parts + [jnp.zeros((1, LANES), F32)] * (8 - len(parts))
+            each = jnp.sum(jnp.concatenate(parts, axis=0), axis=1, keepdims=True)
+            packed = jnp.sum(jnp.where(diagonal, each, 0.0), axis=0, keepdims=True)
             if last is not None:
-                parts[7] = last
-            near_slots[r, near_rank] = jnp.concatenate(parts, axis=0)
+                packed = jnp.where(lane == 7, last, packed)
+            near_slots[r, near_rank] = packed
             for k in range(1, near):
                 near_copy(r, k).start()
 
         def total_of(slots, scaled):
-            t = slots
             if not scaled:
-                return jnp.sum(t, axis=0)
-            scale = t[:, 7:8, :]
+                return jnp.sum(slots, axis=0)
+            t = slots[:, 0, :]
+            scale = t[:, 7:8]
             top = jnp.max(scale, axis=0, keepdims=True)
             ratio = scale / top
-            t = jnp.sum(t * (ratio * ratio), axis=0)
-            keep = lax.broadcasted_iota(jnp.int32, (8, LANES), 0) == 7
-            return jnp.where(keep, jnp.broadcast_to(top[0], (8, LANES)), t)
+            t = jnp.sum(t * (ratio * ratio), axis=0, keepdims=True)
+            return jnp.where(lane == 7, top, t)
 
         def sum_middle(r, scaled=False):
             near_all(r).wait_recv()
@@ -274,8 +279,9 @@
         def sum_end(r, scaled=False):
             far_all(r).wait_recv()
             t = total_of(far_slots[r], scaled)
-            m = jnp.sum(t, axis=1, keepdims=True) * (1.0 / count)
-            return jnp.broadcast_to(m, (8, LANES)), t[7:8, :]
+            m = jnp.sum(jnp.where(diagonal, t, 0.0), axis=1, keepdims=True)
+            m = jnp.broadcast_to(m, (8, LANES))
+            return m * (1.0 / count), m[7:8, :]
 
         def sum_drain(r):
             near_all(r).wait_send()
@@ -357,8 +363,7 @@
         apply_arriving(0, done0)
 
         pl.semaphore_wait(ready.at[1], 2)
-        sum_begin(1, sums, peak)
-        begin(1)
+        begin(1, lambda: sum_begin(1, sums, peak))
         for c in d_copies():
             c.wait_recv()
 
@@ -398,24 +403,29 @@
         r0, v_da0, v_dv0 = k2 * row(t, 1), k2 * row(t, 2), k2 * row(t, 3)
         along0 = v_da0 - r0 * v_dv0
         c0w, r0w, l0w = across(c0), across(r0), across(along0)
-        sums = [jnp.zeros((8, LANES), F32) for _ in range(8)]
         for s in range(sectors):
             di = inverse(s)
             v, a, hd, b = start[s] * c0w, va[s] * c0w, vh[s] * c0w, vb[s] * c0w
             da = a * di
             q = b - r0w * hd - l0w * a
             corr = da - r0w * (v * di) - l0w * v
-            dq, dc = q * di, corr * di
-            put(fields[2], s, dq)
+            put(fields[2], s, q * di)
             start[s], va[s], vh[s], vb[s], vq[s], vc[s] = v, a, hd, b, q, corr
-            new = (
-                corr * corr, corr * a, v * q, corr * q,
-                v * dq + corr * da, corr * dq, v * dc, corr * dc,
-            )
-            sums = [c + fold(n) for c, n in zip(sums, new, strict=True)]
-
-        sum_begin(2, sums)
-        begin(2)
+
+        def sums_of_step():
+            sums = [jnp.zeros((8, LANES), F32) for _ in range(8)]
+            for s in range(sectors):
+                di = inverse(s)
+                v, a, q, corr = start[s], va[s], vq[s], vc[s]
+                da, dq, dc = a * di, q * di, corr * di
+                new = (
+                    corr * corr, corr * a, v * q, corr * q,
+                    v * dq + corr * da, corr * dq, v * dc, corr * dc,
+                )
+                sums = [c + fold(n) for c, n in zip(sums, new, strict=True)]
+            sum_begin(2, sums)
+
+        begin(2, sums_of_step)
 
         def build(s, carry):
             for e in range(ENV):
@@ -533,8 +543,8 @@
             pltpu.VMEM((wide, ENV, rows, LANES), F32),
             pltpu.VMEM((sectors, rows, LANES), F32),
             field, field, field, field, field, field, field, field, field,
-            pltpu.VMEM((3, near, 8, LANES), F32),
-            pltpu.VMEM((3, zs, 8, LANES), F32),
+            pltpu.VMEM((3, near, 1, LANES), F32),
+            pltpu.VMEM((3, zs, 1, LANES), F32),
             dma((6,)),
             dma((3, 2, ENV)), dma((3, 2, ENV)), dma((3, 2, ENV)), dma((3, 2, ENV)),
             dma((3, 2, 4, ENV)),

time: 59.9 us -> 56.9 us (0.950)
  Pallas kernels: 57.8 us -> 54.9 us
    pallas_call x1, Pallas kernels: 57.8 us -> 54.9 us  [local(): pl.pallas_call(kernel, out_shape=(jax.ShapeDtypeStruct((sectors, rows, co...]
where the time goes in v4:
time: 56.9 us; the launch traced here: 56.8 us
  Pallas kernels  54.9 us (96%)
  local copies, waits for them, and re-layouts  1.33 us (2%)
  between operations  0.64 us (1%)
    pallas_call x1, Pallas kernels, local(): pl.pallas_call(kernel, out_shape=(jax.ShapeDtypeStruct((sectors, rows, co...  54.9 us

profile of v4, /device:TPU:1, one launch (start us, length us, event | category | flops | bytes accessed | tf_op | source)
XLA Modules:
  0.0 56.8 jit_solution(10586265336903142670)
XLA Ops:
  0.6 54.9 %shard_map.77 = (f32[4,64,256]{2,1,0:T(8,128)S(1)}, f32[2,128]{1,0:T(2,128)S(1)}) custom-call(s32[16]{0:T(128)} %shifts_hbm.1, s32[2,4]{1,0:T(2,128)} %bitcast.1, f32[4,64,256]{2,1,0:T(8,128)} %wf_hbm.1, f32[4,64]{1,0:T(4,128)} %prec_hbm.1, bf16[4,16,64,256]{3,2,1,0:T(8,128)(2,1)} %left_hbm.1, bf16[4,16,256,256]{3,2,1,0:T(8,128)(2,1)} %right_hbm.1), custom_call_target="tpu_custom_call" | custom-call | tf_op jit(solution)/shard_map/pallas_call | solution.py:525
  55.5 0.6 %slice_reduce_fusion = f32[2]{0:T(128)} fusion(f32[2,128]{1,0:T(2,128)S(1)} %get-tuple-element.5), kind=kLoop, calls=%fused_computation | loop fusion | bytes 16 | tf_op jit(solution)/shard_map/slice | solution.py:559
  56.1 0.7 %copy.9 = f32[4,64,256]{2,1,0:T(8,128)} copy(f32[4,64,256]{2,1,0:T(8,128)S(1)} %get-tuple-element.8) | data formatting | bytes 524288

commit v5 on v4

--- a/solution.py
+++ b/solution.py
@@ -176,12 +176,12 @@
             dst = fields[e][h].at[pl.ds(in_dst, 2), yy(-k)]
             return cp(src, dst, send_sem.at[e, h, 3, k], in_sem.at[e, h, k], (inner, y))
 
-        def begin(e, between=lambda: None):
+        def begin_outer(e):
             for h in halves:
                 for k in ORDER:
                     gather_outer(e, h, k).start()
-            between()
-
+
+        def begin_rest(e):
             @pl.when(has_out)
             def _():
                 for h in halves:
@@ -298,13 +298,21 @@
                 acc = acc + dot(part, right[s, w, h * half : (h + 1) * half, :])
             return acc
 
-        def apply_arriving(e, done):
+        def apply_arriving(e, prepare, settle):
             finish(e, 0)
             for s in range(sectors):
                 tmp[s] = h_half(fields[e], 0, s)
             finish(e, 1)
-            for s in range(sectors):
-                done(s, (tmp[s] + h_half(fields[e], 1, s)) * live[s])
+            for first in (out_src, in_src):
+                for j in range(2):
+                    s = first + j
+                    tmp[s] = (tmp[s] + h_half(fields[e], 1, s)) * live[s]
+                if first is out_src:
+                    prepare()
+                for j in range(2):
+                    settle(first + j, tmp[first + j])
+                if first is out_src:
+                    begin_outer(e + 1)
 
         def apply_built(dst):
             for s in range(sectors):
@@ -312,7 +320,8 @@
             for s in range(sectors):
                 dst[s] = (dst[s] + h_half((xt0, xt1), 1, s)) * live[s]
 
-        begin(0)
+        begin_outer(0)
+        begin_rest(0)
         greet(ready.at[0])
 
         def d_copies():
@@ -360,10 +369,11 @@
             for i, n in enumerate((u * u, u * ua, u * (ua * di), u * (u * di))):
                 sums[i] = sums[i] + fold(n)
 
-        apply_arriving(0, done0)
+        apply_arriving(0, lambda: None, done0)
 
         pl.semaphore_wait(ready.at[1], 2)
-        begin(1, lambda: sum_begin(1, sums, peak))
+        sum_begin(1, sums, peak)
+        begin_rest(1)
         for c in d_copies():
             c.wait_recv()
 
@@ -393,39 +403,39 @@
         sum_middle(1, True)
         pass_inner(1)
 
+        first_step = {}
+
+        def scalars_of_start():
+            t, top = sum_end(1, True)
+            c0 = lax.rsqrt(top * (top * row(t, 0)) + 1e-06)
+            k2 = (c0 * top) * (c0 * top)
+            r0, v_da0, v_dv0 = k2 * row(t, 1), k2 * row(t, 2), k2 * row(t, 3)
+            first_step["scalars"] = c0, r0, v_da0 - r0 * v_dv0, v_da0, v_dv0
+
         def done1(s, b):
-            vb[s] = b
-
-        apply_arriving(1, done1)
-        t, top = sum_end(1, True)
-        c0 = lax.rsqrt(top * (top * row(t, 0)) + 1e-06)
-        k2 = (c0 * top) * (c0 * top)
-        r0, v_da0, v_dv0 = k2 * row(t, 1), k2 * row(t, 2), k2 * row(t, 3)
-        along0 = v_da0 - r0 * v_dv0
-        c0w, r0w, l0w = across(c0), across(r0), across(along0)
+            c0w, r0w, l0w = (across(c) for c in first_step["scalars"][:3])
+            di = inverse(s)
+            v, a, hd, b = start[s] * c0w, va[s] * c0w, vh[s] * c0w, b * c0w
+            q = b - r0w * hd - l0w * a
+            put(fields[2], s, q * di)
+            corr = a * di - r0w * (v * di) - l0w * v
+            start[s], va[s], vh[s], vb[s], vq[s], vc[s] = v, a, hd, b, q, corr
+
+        apply_arriving(1, scalars_of_start, done1)
+        c0, r0, along0, v_da0, v_dv0 = first_step["scalars"]
+
+        sums = [jnp.zeros((8, LANES), F32) for _ in range(8)]
         for s in range(sectors):
             di = inverse(s)
-            v, a, hd, b = start[s] * c0w, va[s] * c0w, vh[s] * c0w, vb[s] * c0w
-            da = a * di
-            q = b - r0w * hd - l0w * a
-            corr = da - r0w * (v * di) - l0w * v
-            put(fields[2], s, q * di)
-            start[s], va[s], vh[s], vb[s], vq[s], vc[s] = v, a, hd, b, q, corr
-
-        def sums_of_step():
-            sums = [jnp.zeros((8, LANES), F32) for _ in range(8)]
-            for s in range(sectors):
-                di = inverse(s)
-                v, a, q, corr = start[s], va[s], vq[s], vc[s]
-                da, dq, dc = a * di, q * di, corr * di
-                new = (
-                    corr * corr, corr * a, v * q, corr * q,
-                    v * dq + corr * da, corr * dq, v * dc, corr * dc,
-                )
-                sums = [c + fold(n) for c, n in zip(sums, new, strict=True)]
-            sum_begin(2, sums)
-
-        begin(2, sums_of_step)
+            v, a, q, corr = start[s], va[s], vq[s], vc[s]
+            da, dq, dc = a * di, q * di, corr * di
+            new = (
+                corr * corr, corr * a, v * q, corr * q,
+                v * dq + corr * da, corr * dq, v * dc, corr * dc,
+            )
+            sums = [c + fold(n) for c, n in zip(sums, new, strict=True)]
+        sum_begin(2, sums)
+        begin_rest(2)
 
         def build(s, carry):
             for e in range(ENV):
@@ -444,10 +454,11 @@
         sum_middle(2)
         pass_inner(2)
 
-        def done2(s, n):
-            tmp[s] = n
-
-        apply_arriving(2, done2)
+        for h in halves:
+            finish(2, h)
+            for s in range(sectors):
+                n = h_half(fields[2], h, s)
+                tmp[s] = n if h == 0 else (tmp[s] + n) * live[s]
         t, _ = sum_end(2)
 
         def rotation(rayleigh, upper, coupling):

time: 56.9 us -> 55.9 us (0.982)
  Pallas kernels: 54.9 us -> 53.9 us
    pallas_call x1, Pallas kernels: 54.9 us -> 53.9 us  [local(): pl.pallas_call(kernel, out_shape=(jax.ShapeDtypeStruct((sectors, rows, co...]
where the time goes in v5:
time: 55.9 us; the launch traced here: 55.8 us
  Pallas kernels  53.9 us (96%)
  local copies, waits for them, and re-layouts  1.33 us (2%)
  between operations  0.64 us (1%)
    pallas_call x1, Pallas kernels, local(): pl.pallas_call(kernel, out_shape=(jax.ShapeDtypeStruct((sectors, rows, co...  53.9 us

profile of v5, /device:TPU:1, one launch (start us, length us, event | category | flops | bytes accessed | tf_op | source)
XLA Modules:
  0.0 55.8 jit_solution(6747755544084885237)
XLA Ops:
  0.6 53.9 %shard_map.77 = (f32[4,64,256]{2,1,0:T(8,128)S(1)}, f32[2,128]{1,0:T(2,128)S(1)}) custom-call(s32[16]{0:T(128)} %shifts_hbm.1, s32[2,4]{1,0:T(2,128)} %bitcast.1, f32[4,64,256]{2,1,0:T(8,128)} %wf_hbm.1, f32[4,64]{1,0:T(4,128)} %prec_hbm.1, bf16[4,16,64,256]{3,2,1,0:T(8,128)(2,1)} %left_hbm.1, bf16[4,16,256,256]{3,2,1,0:T(8,128)(2,1)} %right_hbm.1), custom_call_target="tpu_custom_call" | custom-call | tf_op jit(solution)/shard_map/pallas_call | solution.py:536
  54.5 0.6 %slice_reduce_fusion = f32[2]{0:T(128)} fusion(f32[2,128]{1,0:T(2,128)S(1)} %get-tuple-element.5), kind=kLoop, calls=%fused_computation | loop fusion | bytes 16 | tf_op jit(solution)/shard_map/slice | solution.py:570
  55.1 0.7 %copy.9 = f32[4,64,256]{2,1,0:T(8,128)} copy(f32[4,64,256]{2,1,0:T(8,128)S(1)} %get-tuple-element.8) | data formatting | bytes 524288

commit v6 on v5

--- a/solution.py
+++ b/solution.py
@@ -56,9 +56,15 @@
 
         near_rank = (core * ENV + y) * xs + x
 
+        shifted_x = [lax.rem(x + d, xs) for d in range(xs)]
+        shifted_y = [lax.rem(y + d, ENV) for d in range(ENV)]
+        offsets = [(c, dy, dx) for dx in range(xs) for dy in range(ENV) for c in (0, 1)][1:]
+        offsets.sort(key=lambda o: -(min(o[1], ENV - o[1]) + min(o[2], xs - o[2])))
+
         def near_peer(k):
-            m = lax.rem(near_rank + k, near)
-            return (((lax.rem(m, xs) * zs + z) * 2 + m // (xs * ENV)), lax.rem(m // xs, ENV))
+            c, dy, dx = offsets[k - 1]
+            other = core if c == 0 else 1 - core
+            return ((shifted_x[dx] * zs + z) * 2 + other, shifted_y[dy])
 
         def far_peer(k):
             m = lax.rem(z + k + zs, zs)
@@ -69,6 +75,35 @@
 
         greeted = [(sec, yy(k)) for k in range(1, ENV)] + [(inner, yy(k)) for k in range(ENV)]
         greeted += [x_peer(k) for k in range(1, xs)] + [far_peer(1), far_peer(-1)]
+
+        zero = jnp.zeros((MAXSHIFT, ENV, rows, half), BF)
+        ones = jnp.ones((MAXSHIFT, ENV, 1, LANES), F32)
+
+        @pl.when(sec == 0)
+        def _():
+            for pair in fields:
+                for buf in pair:
+                    buf[0:MAXSHIFT] = zero
+            dall[0:MAXSHIFT] = ones
+
+        @pl.when(sec == nsec - 1)
+        def _():
+            for pair in fields:
+                for buf in pair:
+                    buf[wide - MAXSHIFT : wide] = zero
+            dall[wide - MAXSHIFT : wide] = ones
+
+        def greet(semaphore):
+            for peer in greeted:
+                pl.semaphore_signal(semaphore, inc=1, device_id=peer, device_id_type=MESH)
+
+            @pl.when(has_out)
+            def _():
+                pl.semaphore_signal(semaphore, inc=1, device_id=(outer, y), device_id_type=MESH)
+
+        barrier = pltpu.get_barrier_semaphore()
+        greet(barrier)
+        expected = len(greeted) + jnp.where(has_out, 1, 0)
 
         loads = [
             pltpu.make_async_copy(a, b, load_sem.at[i])
@@ -78,35 +113,6 @@
         ]
         for load in loads:
             load.start()
-
-        zero = jnp.zeros((MAXSHIFT, ENV, rows, half), BF)
-        ones = jnp.ones((MAXSHIFT, ENV, 1, LANES), F32)
-
-        @pl.when(sec == 0)
-        def _():
-            for pair in fields:
-                for buf in pair:
-                    buf[0:MAXSHIFT] = zero
-            dall[0:MAXSHIFT] = ones
-
-        @pl.when(sec == nsec - 1)
-        def _():
-            for pair in fields:
-                for buf in pair:
-                    buf[wide - MAXSHIFT : wide] = zero
-            dall[wide - MAXSHIFT : wide] = ones
-
-        def greet(semaphore):
-            for peer in greeted:
-                pl.semaphore_signal(semaphore, inc=1, device_id=peer, device_id_type=MESH)
-
-            @pl.when(has_out)
-            def _():
-                pl.semaphore_signal(semaphore, inc=1, device_id=(outer, y), device_id_type=MESH)
-
-        barrier = pltpu.get_barrier_semaphore()
-        greet(barrier)
-        expected = len(greeted) + jnp.where(has_out, 1, 0)
 
         for load in loads[:3]:
             load.wait()

time: 55.9 us -> 55.9 us (level)
  no operation moved by 1% of the time
where the time goes in v6:
time: 55.9 us; the launch traced here: 55.8 us
  Pallas kernels  53.9 us (96%)
  local copies, waits for them, and re-layouts  1.33 us (2%)
  between operations  0.64 us (1%)
    pallas_call x1, Pallas kernels, local(): pl.pallas_call(kernel, out_shape=(jax.ShapeDtypeStruct((sectors, rows, co...  53.9 us

profile of v6, /device:TPU:1, one launch (start us, length us, event | category | flops | bytes accessed | tf_op | source)
XLA Modules:
  0.0 55.8 jit_solution(12602185751718130516)
XLA Ops:
  0.6 53.9 %shard_map.77 = (f32[4,64,256]{2,1,0:T(8,128)S(1)}, f32[2,128]{1,0:T(2,128)S(1)}) custom-call(s32[16]{0:T(128)} %shifts_hbm.1, s32[2,4]{1,0:T(2,128)} %bitcast.1, f32[4,64,256]{2,1,0:T(8,128)} %wf_hbm.1, f32[4,64]{1,0:T(4,128)} %prec_hbm.1, bf16[4,16,64,256]{3,2,1,0:T(8,128)(2,1)} %left_hbm.1, bf16[4,16,256,256]{3,2,1,0:T(8,128)(2,1)} %right_hbm.1), custom_call_target="tpu_custom_call" | custom-call | tf_op jit(solution)/shard_map/pallas_call | solution.py:542
  54.5 0.6 %slice_reduce_fusion = f32[2]{0:T(128)} fusion(f32[2,128]{1,0:T(2,128)S(1)} %get-tuple-element.5), kind=kLoop, calls=%fused_computation | loop fusion | bytes 16 | tf_op jit(solution)/shard_map/slice | solution.py:576
  55.1 0.7 %copy.9 = f32[4,64,256]{2,1,0:T(8,128)} copy(f32[4,64,256]{2,1,0:T(8,128)S(1)} %get-tuple-element.8) | data formatting | bytes 524288
